TPU v7x, 256 devices: a whole 4x4x8 slice. The times are simulated.
256 devices in a mesh: azi: 8 (over y, core), rad: 16 (over x, z_lo), axl: 2 (over z_hi).
Axes of the slice: x: 4, y: 4, z: 8 (z_hi: 2, z_lo: 4; z = z_hi * 4 + z_lo), core: 2. Of those that a mesh axis runs over, the one named last changes fastest.
Arguments:
- perturbation: float32 [5, 8, 1024, 2048], P(None, 'axl', 'rad', 'azi'), may hold values from -6 to 6
- axial_velocity: float32 [8, 1024], P('axl', 'rad'), may hold values from 0.4 to 1.2
- swirl_velocity: float32 [8, 1024], P('axl', 'rad'), may hold values from -0.8 to 0.8
- sound_speed: float32 [8, 1024], P('axl', 'rad'), may hold values from 1 to 1.6
- rotor_offset: int32 [1], replicated, may hold values from 0 to 2047
Outputs:
- tendency: float32 [5, 8, 1024, 2048], P(None, 'axl', 'rad', 'azi')
All inputs are finite; a program needn't handle non-finite values.
Results may differ from a plain program's by a relative error of at most 0.000065.
Values sent between devices are 32-bit elements; how exact they have to be, the bound alone decides.
No kernel may reach another device: no remote copies, remote signals or barrier semaphores. Data moves between devices by JAX's collectives and lax.ppermute only.
A program may use at most 128 MiB of HBM per device.

v0:
```python
import jax
import jax.numpy as jnp
import numpy as np
from jax import lax
from jax.sharding import PartitionSpec as P

NA = 2048
BAND = 128
WEIGHTS = (45.0 / 60.0, -9.0 / 60.0, 1.0 / 60.0)


def partner(value, axis, distance):
    mask = 2**distance
    pairs = [(source, source ^ mask) for source in range(lax.axis_size(axis))]
    return lax.ppermute(value, axis, pairs)


def with_halo(block, sides, width):
    for axis, dim in sides:
        count = lax.axis_size(axis)
        forward = [(i, i + 1) for i in range(count - 1)]
        backward = [(target, source) for source, target in forward]
        low = lax.ppermute(
            lax.slice_in_dim(block, block.shape[dim] - width, None, axis=dim), axis, forward
        )
        high = lax.ppermute(lax.slice_in_dim(block, 0, width, axis=dim), axis, backward)
        block = jnp.concatenate([low, block, high], axis=dim)
    return block


def stencil_coefs(cells, reach):
    offsets = np.arange(1, reach + 1)
    signs = np.where(offsets % 2 == 1, 1.0, -1.0)
    angles = np.pi * offsets / cells
    values = np.pi / cells * signs * np.cos(angles) / np.sin(angles)
    return np.concatenate([np.zeros(1), values])


def signed_table(coefs, offsets):
    reach = coefs.shape[0] - 1
    magnitude = np.abs(offsets)
    picked = coefs[np.minimum(magnitude, reach)]
    return np.where(magnitude <= reach, np.sign(offsets) * picked, 0.0)


def band_table(coefs, columns):
    reach = coefs.shape[0] - 1
    source = np.arange(columns + 2 * reach)
    target = np.arange(columns)
    offsets = source[:, None] - target[None, :] - reach
    return signed_table(coefs, offsets)


def central_diff(padded, axis_pos):
    extent = padded.shape[axis_pos] - 6
    result = jnp.zeros_like(lax.slice_in_dim(padded, 3, 3 + extent, axis=axis_pos))
    for reach_k, weight in enumerate(WEIGHTS, start=1):
        upper = lax.slice_in_dim(padded, 3 + reach_k, 3 + reach_k + extent, axis=axis_pos)
        lower = lax.slice_in_dim(padded, 3 - reach_k, 3 - reach_k + extent, axis=axis_pos)
        result = result + weight * (upper - lower)
    return result


def section_terms(padded, angular, axial_vel, swirl_vel, sound_vel, metric):
    deriv_x = central_diff(padded, 1)
    stream = axial_vel[:, :, None]
    turning = (swirl_vel * metric[None, :])[:, :, None]
    speed_sq = (sound_vel * sound_vel)[:, :, None]
    scale = metric[:, None]
    convect = stream * deriv_x + turning * angular
    spread = deriv_x[1] + scale * angular[3]
    return jnp.stack(
        [
            -(convect[0] + spread),
            -(convect[1] + deriv_x[4]),
            -convect[2],
            -(convect[3] + scale * angular[4]),
            -(convect[4] + speed_sq * spread),
        ]
    )


def radial_terms(radial, sound_vel):
    speed_sq = (sound_vel * sound_vel)[:, :, None]
    blank = jnp.zeros_like(radial[0])
    return jnp.stack([-radial[0], blank, -radial[1], blank, -speed_sq * radial[0]])


def make_metric(first_row, row_count, radial_total):
    index = (first_row + jnp.arange(row_count, dtype=jnp.int32)).astype(jnp.float32)
    return 2.0 / (1.0 + (index + 0.5) / radial_total)


def rotate_edge(edge_lines, start_cell):
    doubled = jnp.concatenate([edge_lines, edge_lines], axis=3)
    return lax.dynamic_slice_in_dim(doubled, start_cell, NA, 3)


def attach_planes(values, received, stator_side):
    blanks = jnp.zeros_like(received)
    lower = jnp.where(stator_side, blanks, received)
    upper = jnp.where(stator_side, received, blanks)
    return jnp.concatenate([lower, values, upper], axis=1)


def tiled_lines(lines_all, coefs):
    width = BAND
    blocks = NA // width
    lead = lines_all.shape[:3]
    tiles = lines_all.reshape(lead + (blocks, width))
    banded = band_table(coefs, width)
    left_part = jnp.asarray(banded[0:width], dtype=jnp.float32)
    middle_part = jnp.asarray(banded[width : 2 * width], dtype=jnp.float32)
    right_part = jnp.asarray(banded[2 * width : 3 * width], dtype=jnp.float32)
    form = "fxrke,ej->fxrkj"
    middle = jnp.einsum(
        form,
        tiles,
        middle_part,
        precision=lax.Precision.HIGHEST,
        preferred_element_type=jnp.float32,
    )
    from_left = jnp.einsum(
        form, tiles, left_part, precision=lax.Precision.HIGHEST, preferred_element_type=jnp.float32
    )
    from_right = jnp.einsum(
        form, tiles, right_part, precision=lax.Precision.HIGHEST, preferred_element_type=jnp.float32
    )
    result = middle + jnp.roll(from_left, 1, axis=3) + jnp.roll(from_right, -1, axis=3)
    return result.reshape(lines_all.shape)


def per_device(perturbation, axial_velocity, swirl_velocity, sound_speed, rotor_offset):
    azi_count = lax.axis_size("azi")
    rad_count = lax.axis_size("rad")
    rows = perturbation.shape[2]
    sub_rows = rows // azi_count
    azi_pos = lax.axis_index("azi")
    rad_pos = lax.axis_index("rad")
    axl_pos = lax.axis_index("axl")
    radial_total = rows * rad_count
    coefs = stencil_coefs(NA, BAND)
    shift_cells = rotor_offset[0]
    stator_side = axl_pos == 0
    start_cell = jnp.where(stator_side, shift_cells, NA - shift_cells) % NA
    lines_all = lax.all_to_all(perturbation, "azi", split_axis=2, concat_axis=3, tiled=True)
    angular = tiled_lines(lines_all, coefs)
    edge_lines = jnp.where(stator_side, lines_all[:, -3:], lines_all[:, :3])
    received = partner(rotate_edge(edge_lines, start_cell), "axl", 0)
    padded = attach_planes(lines_all, received, stator_side)
    row_start = azi_pos * sub_rows
    axial_sub = lax.dynamic_slice_in_dim(axial_velocity, row_start, sub_rows, 1)
    swirl_sub = lax.dynamic_slice_in_dim(swirl_velocity, row_start, sub_rows, 1)
    sound_sub = lax.dynamic_slice_in_dim(sound_speed, row_start, sub_rows, 1)
    metric = make_metric(rad_pos * rows + row_start, sub_rows, radial_total)
    partial_lines = section_terms(padded, angular, axial_sub, swirl_sub, sound_sub, metric)
    partial_value = lax.all_to_all(partial_lines, "azi", split_axis=3, concat_axis=2, tiled=True)
    pair = jnp.stack([perturbation[2], perturbation[4]])
    pair_pad = with_halo(pair, (("rad", 2),), 3)
    radial = central_diff(pair_pad, 2)
    return partial_value + radial_terms(radial, sound_speed)


def solution(mesh):
    return jax.shard_map(
        per_device,
        mesh=mesh,
        in_specs=(
            P(None, "axl", "rad", "azi"),
            P("axl", "rad"),
            P("axl", "rad"),
            P("axl", "rad"),
            P(),
        ),
        out_specs=P(None, "axl", "rad", "azi"),
        check_vma=False,
    )
```

profile of v0, /device:TPU:1, one launch (start us, length us, event | category | flops | bytes accessed | tf_op | source)
XLA Modules:
  0.0 211.9 jit_solution(11327305505855242520)
XLA Ops:
  0.0 3.5 %copy.17 = f32[5,4,64,256]{3,0,1,2:T(8,128)} copy(f32[5,4,64,256]{3,2,1,0:T(8,128)} %param.8) | data formatting | bytes 2621440 | tf_op args[0]
  3.5 6.7 %all-to-all-start = ((f32[5,4,64,256]{3,0,1,2:T(8,128)}), f32[5,4,64,256]{3,0,1,2:T(8,128)S(1)}, u32[]{:S(2)}, u32[]{:S(2)}) async-start(f32[5,4,64,256]{3,0,1,2:T(8,128)} %copy.17), calls=%async_computation | async-start | bytes 4194304 | tf_op jit(solution)/shard_map/all_to_all | solution.py:146
  10.2 1.1 fusion.32
  11.4 1.3 collective-permute-start.1
  12.7 4.0 %collective-permute-start.2 = (f32[2,4,3,256]{3,2,1,0:T(4,128)S(1)}, f32[2,4,3,256]{3,2,1,0:T(4,128)S(1)}, u32[]{:S(2)}, u32[]{:S(2)}) collective-permute-start(f32[2,4,3,256]{3,2,1,0:T(4,128)S(1)} %get-tuple-element.16), channel_id=1, source_target_pairs={{0,2},{2,4},{4,6},{6,8},{8,10},{10,12},{12,14},{14,16},{16,18},{18... | collective-permute-start | bytes 73736 | tf_op jit(solution)/shard_map/ppermute | solution.py:23
  17.7 0.9 pad_maximum_fusion.2
  18.6 18.0 %all-to-all-done = f32[5,4,64,256]{3,0,1,2:T(8,128)S(1)} async-done(((f32[5,4,64,256]{3,0,1,2:T(8,128)}), f32[5,4,64,256]{3,0,1,2:T(8,128)S(1)}, u32[]{:S(2)}, u32[]{:S(2)}) %all-to-all-start) | async-done | bytes 1310752 | tf_op jit(solution)/shard_map/all_to_all | solution.py:146
  36.6 1.3 copy-done.1
  37.9 2.4 %copy.25 = f32[5,4,8,8,256]{4,2,3,1,0:T(8,128)S(1)} copy(f32[5,4,8,8,256]{4,0,1,3,2:T(8,128)} %bitcast.54) | data formatting | bytes 2621440 | tf_op jit(solution)/shard_map/all_to_all | solution.py:146
  40.3 1.0 copy-done
  41.5 1.4 reshape.55
  43.0 1.6 fusion.14
  44.5 6.1 %collective-permute-start = (f32[5,3,8,2048]{3,2,1,0:T(8,128)}, f32[5,3,8,2048]{3,2,1,0:T(8,128)}, u32[]{:S(2)}, u32[]{:S(2)}) collective-permute-start(f32[5,3,8,2048]{3,2,1,0:T(8,128)} %fusion.14), channel_id=1, source_target_pairs={{0,1},{1,0},{2,3},{3,2},{4,5},{5,4},{6,7},{7,6},{8,9},{9,8},{10,11... | collective-permute-start | bytes 2949128 | tf_op jit(solution)/shard_map/ppermute | solution.py:15
  50.7 1.2 convolution_bitcast_fusion
  52.7 1.2 convolution_bitcast_fusion.1
  54.0 2.5 %fusion.1 = f32[5,4,8,16,128]{4,3,2,1,0:T(8,128)} fusion(f32[128,128,1,1,1]{1,0,4,3,2:T(8,128)S(1)} %copy-done.4, f32[5,4,8,16,128]{4,3,2,1,0:T(8,128)S(1)} %reshape.55, f32[5,4,8,15,128]{4,3,2,1,0:T(8,128)S(1)} %bitcast.55, f32[5,4,8,1,128]{4,3,2,1,0:T(1,128)S(1)} %slice.161, f32[5,4,8,1,128]{4,3,2,1,0:T(1,128)S(1)} %slice.164, ...), kind=kOutput, calls=%fused_computation.14 | convolution fusion | flops 504627200 | bytes 5308416 | tf_op jit(solution)/shard_map/fxrke,ej->fxrkj/dot_general | solution.py:116
  56.5 1.5 reshape.56
  58.0 1.9 fusion.31
  59.9 1.0 squeeze.7
  60.9 1.7 squeeze.8
  62.6 14.3 %collective-permute-done = f32[5,3,8,2048]{3,2,1,0:T(8,128)} collective-permute-done((f32[5,3,8,2048]{3,2,1,0:T(8,128)}, f32[5,3,8,2048]{3,2,1,0:T(8,128)}, u32[]{:S(2)}, u32[]{:S(2)}) %collective-permute-start) | collective-permute-done | bytes 983072 | tf_op jit(solution)/shard_map/ppermute | solution.py:15
  76.9 1.4 broadcast_select_fusion.1
  78.3 1.1 multiply_add_fusion
  80.6 12.5 %copy.19 = f32[5,4,8,2048]{2,1,0,3:T(4,128)} copy(f32[5,4,8,2048]{3,2,1,0:T(8,128)S(1)} %fusion.22) | data formatting | bytes 2621440 | tf_op jit(solution)/shard_map/stack | solution.py:72
  93.1 26.6 %reshape.60 = f32[8,1,40960]{2,1,0:T(1,128)} reshape(f32[2048,5,4,8]{3,2,1,0:T(4,128)} %bitcast.50) | data formatting | bytes 2621440
  119.8 20.2 %all-to-all-start.1 = ((f32[8,1,40960]{2,1,0:T(1,128)}), f32[8,1,40960]{2,1,0:T(1,128)S(1)}, u32[]{:S(2)}, u32[]{:S(2)}) async-start(f32[8,1,40960]{2,1,0:T(1,128)} %reshape.60), calls=%async_computation.1 | async-start | bytes 2621440 | tf_op jit(solution)/shard_map/all_to_all | solution.py:157
  143.2 0.8 multiply_dynamic-update-slice_fusion
  144.0 13.9 %all-to-all-done.1 = f32[8,1,40960]{2,1,0:T(1,128)S(1)} async-done(((f32[8,1,40960]{2,1,0:T(1,128)}), f32[8,1,40960]{2,1,0:T(1,128)S(1)}, u32[]{:S(2)}, u32[]{:S(2)}) %all-to-all-start.1) | async-done | bytes 1310752 | tf_op jit(solution)/shard_map/all_to_all | solution.py:157
  158.4 3.7 %reduce = f32[8,40960]{1,0:T(8,128)S(1)} reduce(f32[8,1,40960]{2,1,0:T(1,128)S(1)} %all-to-all-done.1, f32[]{:T(128)} %broadcast.89), dimensions={1}, to_apply=%all_to_all.30.reduce_sub_computation | reduce | bytes 2621444 | tf_op jit(solution)/shard_map/all_to_all | solution.py:157
  162.2 32.6 %reshape.61 = f32[2048,5,4,8]{3,2,1,0:T(4,128)} reshape(f32[8,40960]{1,0:T(8,128)S(1)} %reduce) | data formatting | bytes 2621440
  194.8 14.5 %copy.20 = f32[5,4,8,8,256]{4,3,2,1,0:T(8,128)S(1)} copy(f32[5,4,8,8,256]{3,1,0,4,2:T(4,128)} %bitcast.51) | data formatting | bytes 2621440 | tf_op jit(solution)/shard_map/all_to_all | solution.py:157
  209.4 2.6 %bitcast_add_fusion = f32[5,4,64,256]{3,2,1,0:T(8,128)} fusion(f32[5,4,64,256]{3,2,1,0:T(8,128)} %multiply_dynamic-update-slice_fusion, f32[5,4,8,8,256]{4,3,2,1,0:T(8,128)S(1)} %copy.20), kind=kLoop, calls=%fused_computation.29 | loop fusion | flops 327680 | bytes 3932160 | tf_op jit(solution)/shard_map/add | solution.py:161
  (41 shorter events, 6.4 us)
Async XLA Ops:
  3.5 33.1 %all-to-all-start = ((f32[5,4,64,256]{3,0,1,2:T(8,128)}), f32[5,4,64,256]{3,0,1,2:T(8,128)S(1)}, u32[]{:S(2)}, u32[]{:S(2)}) async-start(f32[5,4,64,256]{3,0,1,2:T(8,128)} %copy.17), calls=%async_computation | async-start | bytes 4194304 | tf_op jit(solution)/shard_map/all_to_all | solution.py:146
  10.2 6.5 %copy-start.7 = (f32[4,64]{1,0:T(4,128)S(1)}, f32[4,64]{1,0:T(4,128)}, u32[]{:S(2)}) copy-start(f32[4,64]{1,0:T(4,128)} %param.11) | copy-start | bytes 3076
  10.2 6.5 %copy-start.8 = (f32[4,64]{1,0:T(4,128)S(1)}, f32[4,64]{1,0:T(4,128)}, u32[]{:S(2)}) copy-start(f32[4,64]{1,0:T(4,128)} %param.10) | copy-start | bytes 3076
  10.2 6.5 %copy-start.9 = (f32[4,64]{1,0:T(4,128)S(1)}, f32[4,64]{1,0:T(4,128)}, u32[]{:S(2)}) copy-start(f32[4,64]{1,0:T(4,128)} %param.9) | copy-start | bytes 3076
  11.4 6.2 %collective-permute-start.1 = (f32[2,4,3,256]{3,2,1,0:T(4,128)S(1)}, f32[2,4,3,256]{3,2,1,0:T(4,128)S(1)}, u32[]{:S(2)}, u32[]{:S(2)}) collective-permute-start(f32[2,4,3,256]{3,2,1,0:T(4,128)S(1)} %get-tuple-element.15), channel_id=1, source_target_pairs={{2,0},{4,2},{6,4},{8,6},{10,8},{12,10},{14,12},{16,14},{18,16},{20... | collective-permute-start | bytes 73736 | tf_op jit(solution)/shard_map/ppermute | solution.py:26
  12.7 5.0 %collective-permute-start.2 = (f32[2,4,3,256]{3,2,1,0:T(4,128)S(1)}, f32[2,4,3,256]{3,2,1,0:T(4,128)S(1)}, u32[]{:S(2)}, u32[]{:S(2)}) collective-permute-start(f32[2,4,3,256]{3,2,1,0:T(4,128)S(1)} %get-tuple-element.16), channel_id=1, source_target_pairs={{0,2},{2,4},{4,6},{6,8},{8,10},{10,12},{12,14},{14,16},{16,18},{18... | collective-permute-start | bytes 73736 | tf_op jit(solution)/shard_map/ppermute | solution.py:23
  36.6 1.3 copy-start.1
  40.2 1.1 copy-start
  43.0 7.7 %copy-start.6 = (f32[128,128,1,1,1]{1,0,4,3,2:T(8,128)S(1)}, f32[128,128,1,1,1]{1,0,4,3,2:T(8,128)}, u32[]{:S(2)}) copy-start(f32[128,128,1,1,1]{1,0,4,3,2:T(8,128)} %constant.66) | copy-start | bytes 196612
  44.5 32.3 %collective-permute-start = (f32[5,3,8,2048]{3,2,1,0:T(8,128)}, f32[5,3,8,2048]{3,2,1,0:T(8,128)}, u32[]{:S(2)}, u32[]{:S(2)}) collective-permute-start(f32[5,3,8,2048]{3,2,1,0:T(8,128)} %fusion.14), channel_id=1, source_target_pairs={{0,1},{1,0},{2,3},{3,2},{4,5},{5,4},{6,7},{7,6},{8,9},{9,8},{10,11... | collective-permute-start | bytes 2949128 | tf_op jit(solution)/shard_map/ppermute | solution.py:15
  51.8 0.8 copy-start.5
  52.7 1.3 copy-start.4
  79.4 1.0 copy-start.3
  119.8 20.2 %copy-start.2 = (f32[2,4,67,256]{3,2,1,0:T(8,128)S(1)}, f32[2,4,67,256]{3,2,1,0:T(8,128)}, u32[]{:S(2)}) copy-start(f32[2,4,67,256]{3,2,1,0:T(8,128)} %get-tuple-element.14) | copy-start | bytes 1646596
  119.8 38.1 %all-to-all-start.1 = ((f32[8,1,40960]{2,1,0:T(1,128)}), f32[8,1,40960]{2,1,0:T(1,128)S(1)}, u32[]{:S(2)}, u32[]{:S(2)}) async-start(f32[8,1,40960]{2,1,0:T(1,128)} %reshape.60), calls=%async_computation.1 | async-start | bytes 2621440 | tf_op jit(solution)/shard_map/all_to_all | solution.py:157
where the time goes:
time: 213 us; the launch traced here: 212 us
  local copies, waits for them, and re-layouts  107 us (50%)
  waiting for transfers between devices  46.3 us (22%)
  starting transfers between devices  38.4 us (18%)
  other arithmetic  14.5 us (7%)
  matrix products  4.92 us (2%)
    unnamed x25, local copies, waits for them, and re-layouts  68 us
    all_to_all x1, starting transfers between devices, per_device(): lax.all_to_all(partial_lines, 'azi', split_axis=3, concat_axis=2, tiled=T...  20.2 us
    all_to_all x1, waiting for transfers between devices, per_device(): lax.all_to_all(perturbation, 'azi', split_axis=2, concat_axis=3, tiled=True)  18 us
    all_to_all x2, local copies, waits for them, and re-layouts, per_device(): lax.all_to_all(partial_lines, 'azi', split_axis=3, concat_axis=2, tiled=T...  15.1 us
    ppermute x1, waiting for transfers between devices, partner(): return lax.ppermute(value, axis, pairs)  14.3 us
    all_to_all x1, waiting for transfers between devices, per_device(): lax.all_to_all(partial_lines, 'azi', split_axis=3, concat_axis=2, tiled=T...  13.9 us
    another operation x1, local copies, waits for them, and re-layouts, section_terms(): jnp.stack([-(convect[0] + spread), -(convect[1] + deriv_x[4]), -convect[2...  12.5 us
    all_to_all x1, starting transfers between devices, per_device(): lax.all_to_all(perturbation, 'azi', split_axis=2, concat_axis=3, tiled=True)  6.74 us
  transfers between devices with their start and end apart: 5, of which 4 were waited for; matrix products, arithmetic and copies ran while one was open for 8% of the time, Pallas kernels for 0%

commit v1 on v0

--- a/solution.py
+++ b/solution.py
@@ -143,7 +143,12 @@
     shift_cells = rotor_offset[0]
     stator_side = axl_pos == 0
     start_cell = jnp.where(stator_side, shift_cells, NA - shift_cells) % NA
-    lines_all = lax.all_to_all(perturbation, "azi", split_axis=2, concat_axis=3, tiled=True)
+    lines_all = jnp.concatenate(
+        lax.all_to_all(
+            jnp.stack(jnp.split(perturbation, lax.axis_size("azi"), axis=2)), "azi", 0, 0
+        ),
+        axis=3,
+    )
     angular = tiled_lines(lines_all, coefs)
     edge_lines = jnp.where(stator_side, lines_all[:, -3:], lines_all[:, :3])
     received = partner(rotate_edge(edge_lines, start_cell), "axl", 0)

time: 213 us -> 205 us (0.962)
  waiting for transfers between devices: 46.3 us -> 35.8 us
    all_to_all x1, waiting for transfers between devices: 18 us -> 10.6 us  [per_device(): lax.all_to_all(jnp.stack(jnp.split(perturbation, lax.axis_size('azi'), ax...]
    unnamed x25 -> x29, local copies, waits for them, and re-layouts: 68 us -> 71.5 us
    ppermute x1, waiting for transfers between devices: 14.3 us -> 11.1 us  [partner(): return lax.ppermute(value, axis, pairs)]
    all_to_all x2 -> x0, local copies, waits for them, and re-layouts: 2.55 us -> none  [per_device(): lax.all_to_all(perturbation, 'azi', split_axis=2, concat_axis=3, tiled=True)]
  transfers between devices with their start and end apart: 5 -> 5, of which waited for: 4 -> 4; matrix products, arithmetic and copies ran while one was open for 8% -> 10% of each run, Pallas kernels for 0% -> 0%
where the time goes in v1:
time: 205 us; the launch traced here: 204 us
  local copies, waits for them, and re-layouts  109 us (53%)
  starting transfers between devices  38.3 us (19%)
  waiting for transfers between devices  35.8 us (17%)
  other arithmetic  14.5 us (7%)
  matrix products  4.85 us (2%)
    unnamed x29, local copies, waits for them, and re-layouts  71.5 us
    all_to_all x1, starting transfers between devices, per_device(): lax.all_to_all(partial_lines, 'azi', split_axis=3, concat_axis=2, tiled=T...  20.2 us
    all_to_all x2, local copies, waits for them, and re-layouts, per_device(): lax.all_to_all(partial_lines, 'azi', split_axis=3, concat_axis=2, tiled=T...  15.1 us
    all_to_all x1, waiting for transfers between devices, per_device(): lax.all_to_all(partial_lines, 'azi', split_axis=3, concat_axis=2, tiled=T...  13.9 us
    another operation x1, local copies, waits for them, and re-layouts, section_terms(): jnp.stack([-(convect[0] + spread), -(convect[1] + deriv_x[4]), -convect[2...  12.6 us
    ppermute x1, waiting for transfers between devices, partner(): return lax.ppermute(value, axis, pairs)  11.1 us
    all_to_all x1, waiting for transfers between devices, per_device(): lax.all_to_all(jnp.stack(jnp.split(perturbation, lax.axis_size('azi'), ax...  10.6 us
    all_to_all x1, starting transfers between devices, per_device(): lax.all_to_all(jnp.stack(jnp.split(perturbation, lax.axis_size('azi'), ax...  6.71 us
  transfers between devices with their start and end apart: 5, of which 4 were waited for; matrix products, arithmetic and copies ran while one was open for 10% of the time, Pallas kernels for 0%

profile of v1, /device:TPU:1, one launch (start us, length us, event | category | flops | bytes accessed | tf_op | source)
XLA Modules:
  0.0 203.9 jit_solution(10470136314520981554)
XLA Ops:
  0.0 1.7 bitcast_dynamic-update-slice_fusion.7
  1.7 1.6 bitcast_dynamic-update-slice_fusion.6
  3.3 1.6 bitcast_dynamic-update-slice_fusion.5
  4.9 1.6 bitcast_dynamic-update-slice_fusion.4
  6.5 1.6 bitcast_dynamic-update-slice_fusion.3
  10.1 6.7 %all-to-all-start = ((f32[8,5,4,8,256]{4,3,2,1,0:T(8,128)}), f32[8,5,4,8,256]{4,3,2,1,0:T(8,128)S(1)}, u32[]{:S(2)}, u32[]{:S(2)}) async-start(f32[8,5,4,8,256]{4,3,2,1,0:T(8,128)} %bitcast_dynamic-update-slice_fusion), calls=%async_computation | async-start | bytes 2621440 | tf_op jit(solution)/shard_map/all_to_all | solution.py:147
  16.9 1.3 collective-permute-start.1
  18.2 4.0 %collective-permute-start.2 = (f32[2,4,3,256]{3,2,1,0:T(4,128)S(1)}, f32[2,4,3,256]{3,2,1,0:T(4,128)S(1)}, u32[]{:S(2)}, u32[]{:S(2)}) collective-permute-start(f32[2,4,3,256]{3,2,1,0:T(4,128)S(1)} %get-tuple-element.16), channel_id=1, source_target_pairs={{0,2},{2,4},{4,6},{6,8},{8,10},{10,12},{12,14},{14,16},{16,18},{18... | collective-permute-start | bytes 73736 | tf_op jit(solution)/shard_map/ppermute | solution.py:23
  23.2 0.9 pad_maximum_fusion.2
  24.1 10.6 %all-to-all-done = f32[8,5,4,8,256]{4,3,2,1,0:T(8,128)S(1)} async-done(((f32[8,5,4,8,256]{4,3,2,1,0:T(8,128)}), f32[8,5,4,8,256]{4,3,2,1,0:T(8,128)S(1)}, u32[]{:S(2)}, u32[]{:S(2)}) %all-to-all-start) | async-done | bytes 1310752 | tf_op jit(solution)/shard_map/all_to_all | solution.py:147
  35.0 1.5 fusion.13
  36.6 6.1 %collective-permute-start = (f32[5,3,8,2048]{3,2,1,0:T(8,128)}, f32[5,3,8,2048]{3,2,1,0:T(8,128)}, u32[]{:S(2)}, u32[]{:S(2)}) collective-permute-start(f32[5,3,8,2048]{3,2,1,0:T(8,128)} %fusion.13), channel_id=1, source_target_pairs={{0,1},{1,0},{2,3},{3,2},{4,5},{5,4},{6,7},{7,6},{8,9},{9,8},{10,11... | collective-permute-start | bytes 2949128 | tf_op jit(solution)/shard_map/ppermute | solution.py:15
  42.7 1.8 copy.12
  44.5 1.4 reshape_reshape.3
  45.9 1.2 fusion.33
  47.9 1.2 fusion.32
  49.2 2.5 %fusion = f32[5,4,8,16,128]{4,3,2,1,0:T(8,128)} fusion(f32[5,4,8,16,128]{4,3,2,1,0:T(8,128)S(1)} %reshape_reshape.3, f32[128,128,1,1,1]{1,0,4,3,2:T(8,128)S(1)} %copy-done.3, f32[5,4,8,15,128]{4,3,2,1,0:T(8,128)S(1)} %bitcast.59, f32[5,4,8,1,128]{4,3,2,1,0:T(1,128)S(1)} %slice.161, f32[5,4,8,1,128]{4,3,2,1,0:T(1,128)S(1)} %slice.164, ...), kind=kOutput, calls=%fused_computation.11 | convolution fusion | flops 504627200 | bytes 5308416 | tf_op jit(solution)/shard_map/fxrke,ej->fxrkj/dot_general | solution.py:116
  51.7 1.5 reshape.59
  53.2 1.9 fusion.30
  55.1 1.0 squeeze.7
  56.1 1.7 squeeze.8
  57.8 11.1 %collective-permute-done = f32[5,3,8,2048]{3,2,1,0:T(8,128)} collective-permute-done((f32[5,3,8,2048]{3,2,1,0:T(8,128)}, f32[5,3,8,2048]{3,2,1,0:T(8,128)}, u32[]{:S(2)}, u32[]{:S(2)}) %collective-permute-start) | collective-permute-done | bytes 983072 | tf_op jit(solution)/shard_map/ppermute | solution.py:15
  68.9 1.4 broadcast_select_fusion.1
  70.4 1.1 multiply_add_fusion
  72.6 12.6 %copy.14 = f32[5,4,8,2048]{2,1,0,3:T(4,128)} copy(f32[5,4,8,2048]{3,2,1,0:T(8,128)S(1)} %fusion.21) | data formatting | bytes 2621440 | tf_op jit(solution)/shard_map/stack | solution.py:72
  85.2 26.6 %reshape.63 = f32[8,1,40960]{2,1,0:T(1,128)} reshape(f32[2048,5,4,8]{3,2,1,0:T(4,128)} %bitcast.53) | data formatting | bytes 2621440
  111.9 20.2 %all-to-all-start.1 = ((f32[8,1,40960]{2,1,0:T(1,128)}), f32[8,1,40960]{2,1,0:T(1,128)S(1)}, u32[]{:S(2)}, u32[]{:S(2)}) async-start(f32[8,1,40960]{2,1,0:T(1,128)} %reshape.63), calls=%async_computation.1 | async-start | bytes 2621440 | tf_op jit(solution)/shard_map/all_to_all | solution.py:162
  136.1 13.9 %all-to-all-done.1 = f32[8,1,40960]{2,1,0:T(1,128)S(1)} async-done(((f32[8,1,40960]{2,1,0:T(1,128)}), f32[8,1,40960]{2,1,0:T(1,128)S(1)}, u32[]{:S(2)}, u32[]{:S(2)}) %all-to-all-start.1) | async-done | bytes 1310752 | tf_op jit(solution)/shard_map/all_to_all | solution.py:162
  150.5 3.7 %reduce = f32[8,40960]{1,0:T(8,128)S(1)} reduce(f32[8,1,40960]{2,1,0:T(1,128)S(1)} %all-to-all-done.1, f32[]{:T(128)} %broadcast.89), dimensions={1}, to_apply=%all_to_all.17.reduce_sub_computation | reduce | bytes 2621444 | tf_op jit(solution)/shard_map/all_to_all | solution.py:162
  154.2 32.6 %reshape.64 = f32[2048,5,4,8]{3,2,1,0:T(4,128)} reshape(f32[8,40960]{1,0:T(8,128)S(1)} %reduce) | data formatting | bytes 2621440
  186.8 14.5 %copy.15 = f32[5,4,8,8,256]{4,3,2,1,0:T(8,128)S(1)} copy(f32[5,4,8,8,256]{3,1,0,4,2:T(4,128)} %bitcast.54) | data formatting | bytes 2621440 | tf_op jit(solution)/shard_map/all_to_all | solution.py:162
  201.3 2.6 %bitcast_add_fusion = f32[5,4,64,256]{3,2,1,0:T(8,128)} fusion(f32[5,4,64,256]{3,2,1,0:T(8,128)} %multiply_dynamic-update-slice_fusion, f32[5,4,8,8,256]{4,3,2,1,0:T(8,128)S(1)} %copy.15), kind=kLoop, calls=%fused_computation.26 | loop fusion | flops 327680 | bytes 3932160 | tf_op jit(solution)/shard_map/add | solution.py:166
  (46 shorter events, 9.2 us)
Async XLA Ops:
  0.0 8.1 %copy-start.1 = (f32[5,4,64,256]{3,2,1,0:T(8,128)S(1)}, f32[5,4,64,256]{3,2,1,0:T(8,128)}, u32[]{:S(2)}) copy-start(f32[5,4,64,256]{3,2,1,0:T(8,128)} %param.8) | copy-start | bytes 3932164
  10.1 24.6 %all-to-all-start = ((f32[8,5,4,8,256]{4,3,2,1,0:T(8,128)}), f32[8,5,4,8,256]{4,3,2,1,0:T(8,128)S(1)}, u32[]{:S(2)}, u32[]{:S(2)}) async-start(f32[8,5,4,8,256]{4,3,2,1,0:T(8,128)} %bitcast_dynamic-update-slice_fusion), calls=%async_computation | async-start | bytes 2621440 | tf_op jit(solution)/shard_map/all_to_all | solution.py:147
  16.8 5.4 %copy-start.6 = (f32[4,64]{1,0:T(4,128)S(1)}, f32[4,64]{1,0:T(4,128)}, u32[]{:S(2)}) copy-start(f32[4,64]{1,0:T(4,128)} %param.11) | copy-start | bytes 3076
  16.8 5.4 %copy-start.7 = (f32[4,64]{1,0:T(4,128)S(1)}, f32[4,64]{1,0:T(4,128)}, u32[]{:S(2)}) copy-start(f32[4,64]{1,0:T(4,128)} %param.10) | copy-start | bytes 3076
  16.8 5.4 %copy-start.8 = (f32[4,64]{1,0:T(4,128)S(1)}, f32[4,64]{1,0:T(4,128)}, u32[]{:S(2)}) copy-start(f32[4,64]{1,0:T(4,128)} %param.9) | copy-start | bytes 3076
  16.9 6.2 %collective-permute-start.1 = (f32[2,4,3,256]{3,2,1,0:T(4,128)S(1)}, f32[2,4,3,256]{3,2,1,0:T(4,128)S(1)}, u32[]{:S(2)}, u32[]{:S(2)}) collective-permute-start(f32[2,4,3,256]{3,2,1,0:T(4,128)S(1)} %get-tuple-element.15), channel_id=1, source_target_pairs={{2,0},{4,2},{6,4},{8,6},{10,8},{12,10},{14,12},{16,14},{18,16},{20... | collective-permute-start | bytes 73736 | tf_op jit(solution)/shard_map/ppermute | solution.py:26
  18.2 5.0 %collective-permute-start.2 = (f32[2,4,3,256]{3,2,1,0:T(4,128)S(1)}, f32[2,4,3,256]{3,2,1,0:T(4,128)S(1)}, u32[]{:S(2)}, u32[]{:S(2)}) collective-permute-start(f32[2,4,3,256]{3,2,1,0:T(4,128)S(1)} %get-tuple-element.16), channel_id=1, source_target_pairs={{0,2},{2,4},{4,6},{6,8},{8,10},{10,12},{12,14},{14,16},{16,18},{18... | collective-permute-start | bytes 73736 | tf_op jit(solution)/shard_map/ppermute | solution.py:23
  36.6 32.4 %collective-permute-start = (f32[5,3,8,2048]{3,2,1,0:T(8,128)}, f32[5,3,8,2048]{3,2,1,0:T(8,128)}, u32[]{:S(2)}, u32[]{:S(2)}) collective-permute-start(f32[5,3,8,2048]{3,2,1,0:T(8,128)} %fusion.13), channel_id=1, source_target_pairs={{0,1},{1,0},{2,3},{3,2},{4,5},{5,4},{6,7},{7,6},{8,9},{9,8},{10,11... | collective-permute-start | bytes 2949128 | tf_op jit(solution)/shard_map/ppermute | solution.py:15
  44.5 1.4 copy-start.5
  47.1 0.8 copy-start.4
  47.9 1.3 copy-start.3
  71.5 1.0 copy-start.2
  111.9 20.2 %copy-start = (f32[2,4,67,256]{3,2,1,0:T(8,128)S(1)}, f32[2,4,67,256]{3,2,1,0:T(8,128)}, u32[]{:S(2)}) copy-start(f32[2,4,67,256]{3,2,1,0:T(8,128)} %get-tuple-element.14) | copy-start | bytes 1646596
  111.9 38.1 %all-to-all-start.1 = ((f32[8,1,40960]{2,1,0:T(1,128)}), f32[8,1,40960]{2,1,0:T(1,128)S(1)}, u32[]{:S(2)}, u32[]{:S(2)}) async-start(f32[8,1,40960]{2,1,0:T(1,128)} %reshape.63), calls=%async_computation.1 | async-start | bytes 2621440 | tf_op jit(solution)/shard_map/all_to_all | solution.py:162
